TPU v7x, 32 devices: a whole 2x2x4 slice. The times are simulated.
32 devices in a mesh: row: 8 (over z, core), col: 4 (over y, x).
Axes of the slice: x: 2, y: 2, z: 4, core: 2. Of those that a mesh axis runs over, the one named last changes fastest.
Arguments:
- tokens: bfloat16 [1024, 6144], P('col', 'row'), may hold values from -6 to 6
- up_latent: bfloat16 [6144, 24576], P('row', 'col'), may hold values from -1.0206207 to 1.0206207
- down_latent: bfloat16 [24576, 6144], P('col', 'row'), may hold values from -0.51031036 to 0.51031036
- out_grad: bfloat16 [1024, 6144], P('col', 'row'), may hold values from -6 to 6
Outputs:
- output: bfloat16 [1024, 6144], P('col', 'row')
- in_grad: bfloat16 [1024, 6144], P('col', 'row')
- up_grad: bfloat16 [6144, 24576], P('row', 'col')
- down_grad: bfloat16 [24576, 6144], P('col', 'row')
All inputs are finite; a program needn't handle non-finite values.
Results may differ from a plain program's by a relative error of at most 0.028.
Values may be sent and summed in bfloat16 or wider, within the bound.
A program may use at most 128 MiB of HBM per device.

v0:
```python
import math

import jax
import jax.numpy as jnp
from jax import lax
from jax.sharding import PartitionSpec as P

gelu_coef = math.sqrt(2.0 / math.pi)


def gelu_value(values):
    tanh_arg = gelu_coef * (values + 0.044715 * values * values * values)
    return 0.5 * values * (1.0 + jnp.tanh(tanh_arg))


def gelu_slope(values):
    tanh_val = jnp.tanh(gelu_coef * (values + 0.044715 * values * values * values))
    return 0.5 * (1.0 + tanh_val) + 0.5 * values * (1.0 - tanh_val * tanh_val) * gelu_coef * (
        1.0 + 3.0 * 0.044715 * values * values
    )


def ternary(latent, fan_in):
    limit = 0.8 * fan_in ** (-0.5)
    wide = latent.astype(jnp.float32)
    upper = jnp.where(wide > limit, 1.0, 0.0)
    lower = jnp.where(wide < -limit, 1.0, 0.0)
    return (upper - lower).astype(jnp.bfloat16)


def contract_last(left, right):
    return lax.dot_general(
        left, right, (((1,), (1,)), ((), ())), preferred_element_type=jnp.float32
    )


def contract_first(left, right):
    return lax.dot_general(
        left, right, (((0,), (0,)), ((), ())), preferred_element_type=jnp.float32
    )


def body(tokens, up_latent, down_latent, out_grad):
    rows_axis = lax.axis_size("row")
    cols_axis = lax.axis_size("col")
    entry_total = up_latent.shape[0] * rows_axis * up_latent.shape[1] * cols_axis
    scale_sums = lax.psum(
        (
            jnp.sum(jnp.abs(up_latent.astype(jnp.float32))),
            jnp.sum(jnp.abs(down_latent.astype(jnp.float32))),
        ),
        ("row", "col"),
    )
    up_scale = scale_sums[0] / entry_total
    down_scale = scale_sums[1] / entry_total
    up_tern = ternary(up_latent, up_latent.shape[0] * rows_axis)
    down_tern = ternary(down_latent, down_latent.shape[0] * cols_axis)
    tok_panel, grad_panel = (
        lax.all_gather(tokens, "col", axis=0, tiled=True),
        lax.all_gather(out_grad, "col", axis=0, tiled=True),
    )
    token_total = tok_panel.shape[0]
    grad_norm = 1.0 / math.sqrt(token_total)
    sliced = tok_panel
    hidden = lax.psum_scatter(
        (up_scale * jnp.dot(sliced, up_tern, preferred_element_type=jnp.float32)).astype(
            jnp.bfloat16
        ),
        "row",
        scatter_dimension=0,
        tiled=True,
    ).astype(jnp.float32)
    act_share = gelu_value(hidden).astype(jnp.bfloat16)
    act_panel = lax.all_gather(act_share, "row", axis=0, tiled=True)
    sliced = act_panel
    output = lax.psum_scatter(
        (down_scale * jnp.dot(sliced, down_tern, preferred_element_type=jnp.float32)).astype(
            jnp.bfloat16
        ),
        "col",
        scatter_dimension=0,
        tiled=True,
    )
    down_grad = (contract_first(act_panel, grad_panel) * grad_norm).astype(jnp.bfloat16)
    sliced = grad_panel
    act_grad = lax.psum_scatter(
        (down_scale * contract_last(sliced, down_tern)).astype(jnp.bfloat16),
        "row",
        scatter_dimension=0,
        tiled=True,
    ).astype(jnp.float32)
    hidden_grad = (act_grad * gelu_slope(hidden)).astype(jnp.bfloat16)
    grad_hidden_panel = lax.all_gather(hidden_grad, "row", axis=0, tiled=True)
    up_grad = (contract_first(tok_panel, grad_hidden_panel) * grad_norm).astype(jnp.bfloat16)
    sliced = grad_hidden_panel
    in_grad = lax.psum_scatter(
        (up_scale * contract_last(sliced, up_tern)).astype(jnp.bfloat16),
        "col",
        scatter_dimension=0,
        tiled=True,
    )
    return (output, in_grad, up_grad, down_grad)


def solution(mesh):
    in_specs = (P("col", "row"), P("row", "col"), P("col", "row"), P("col", "row"))
    out_specs = (P("col", "row"), P("col", "row"), P("row", "col"), P("col", "row"))
    return jax.shard_map(body, mesh=mesh, in_specs=in_specs, out_specs=out_specs, check_vma=False)
```

profile of v0, /device:TPU:0, one launch (start us, length us, event | category | flops | bytes accessed | tf_op | source)
XLA Modules:
  0.0 672.3 jit_solution(10110870655289318909)
XLA Ops:
  7.2 0.0 all-gather.5.cloned.1.call-start
  7.2 0.7 all-gather.5.cloned.1.call-update
  7.9 0.0 all-gather.9.cloned.1.call-start
  8.0 9.3 %fusion = f32[]{:T(128)} fusion(bf16[6144,768]{1,0:T(8,128)(2,1)} %param.6), kind=kLoop, calls=%fused_computation.8 | loop fusion | flops 14155775 | bytes 9437188 | tf_op jit(solution)/shard_map/reduce_sum | solution.py:50
  17.2 5.4 fusion.1
  22.7 0.0 reduce-scatter.13.cloned.1.call-start
  22.8 42.8 %all-reduce = (f32[]{:T(128)}, f32[]{:T(128)}) all-reduce(f32[]{:T(128)} %fusion.1, f32[]{:T(128)} %fusion), channel_id=1, replica_groups=mesh['row'=8,'col'=4] {'row','col'}, use_global_device_ids=true, to_apply=%region_3.0 | all-reduce | flops 2 | bytes 16 | tf_op jit(solution)/shard_map/psum | solution.py:47
  66.2 0.0 all-gather.5.cloned.1.call-done
  66.2 16.9 %fusion.2 = bf16[1024,6144]{0,1:T(8,128)(2,1)} fusion(bf16[1024,768]{1,0:T(8,128)(2,1)} %all-gather.5.cloned.1.call-done, f32[]{:T(128)S(6)} %div.7, bf16[768,6144]{1,0:T(8,128)(2,1)} %param.5), kind=kOutput, calls=%fused_computation.14 | convolution fusion | flops 9709289472 | bytes 23592964 | tf_op jit(solution)/shard_map/dot_general | solution.py:66
  83.2 16.6 %copy.10 = bf16[1024,6144]{1,0:T(8,128)(2,1)} copy(bf16[1024,6144]{0,1:T(8,128)(2,1)} %fusion.2) | data formatting | bytes 25165824
  99.8 0.6 reduce-scatter.15.cloned.1.call-start
  101.1 0.0 all-gather.9.cloned.1.call-done
  101.1 16.4 %fusion.3 = bf16[1024,6144]{0,1:T(8,128)(2,1)} fusion(bf16[1024,768]{1,0:T(8,128)(2,1)} %all-gather.9.cloned.1.call-done, f32[]{:T(128)S(6)} %div.6, bf16[6144,768]{1,0:T(8,128)(2,1)} %param.6), kind=kOutput, calls=%fused_computation.15 | convolution fusion | flops 9709289472 | bytes 23592964 | tf_op jit(solution)/shard_map/dot_general | solution.py:32
  117.6 16.8 %copy.12 = bf16[1024,6144]{1,0:T(8,128)(2,1)} copy(bf16[1024,6144]{0,1:T(8,128)(2,1)} %fusion.3) | data formatting | bytes 25165824
  134.3 0.0 all-gather.11.cloned.1.call-start
  134.4 95.2 %reduce-scatter.13.cloned.1.call-done = bf16[128,6144]{1,0:T(8,128)(2,1)} async-done(((bf16[1024,6144]{1,0:T(8,128)(2,1)}), bf16[128,6144]{1,0:T(8,128)(2,1)}) %reduce-scatter.13.cloned.1.call-update) | async-done | bytes 1572880
  229.6 1.9 copy.11
  231.5 127.9 %reduce-scatter.15.cloned.1.call-done = bf16[128,6144]{1,0:T(8,128)(2,1)} async-done(((bf16[1024,6144]{1,0:T(8,128)(2,1)}), bf16[128,6144]{1,0:T(8,128)(2,1)}) %reduce-scatter.15.cloned.1.call-update) | async-done | bytes 1572880
  359.4 1.9 copy.13
  361.3 3.6 fusion.14
  364.9 0.0 all-gather.7.cloned.1.call-start
  365.0 0.5 all-gather.7.cloned.1.call-update
  365.5 0.2 reduce-scatter.11.cloned.1.call-start
  365.7 114.9 %all-gather.11.cloned.1.call-done = bf16[1024,6144]{0,1:T(8,128)(2,1)} async-done(((bf16[128,6144]{0,1:T(8,128)(2,1)}), bf16[1024,6144]{0,1:T(8,128)(2,1)}) %all-gather.11.cloned.1.call-update) | async-done | bytes 12582928 | tf_op jit(solution)/shard_map/all_gather | solution.py:93
  480.6 16.7 %multiply_convert_fusion.4 = bf16[1024,768]{1,0:T(8,128)(2,1)} fusion(bf16[1024,6144]{0,1:T(8,128)(2,1)} %all-gather.11.cloned.1.call-done, bf16[768,6144]{1,0:T(8,128)(2,1)} %param.5, f32[]{:T(128)S(6)} %div.7), kind=kOutput, calls=%fused_computation.37 | convolution fusion | flops 9698279424 | bytes 23592964 | tf_op jit(solution)/shard_map/dot_general | solution.py:32
  497.3 0.3 reduce-scatter.9.cloned.1.call-start
  497.6 100.4 %all-gather.7.cloned.1.call-done = bf16[1024,6144]{0,1:T(8,128)(2,1)} async-done(((bf16[128,6144]{0,1:T(8,128)(2,1)}), bf16[1024,6144]{0,1:T(8,128)(2,1)}) %all-gather.7.cloned.1.call-update) | async-done | bytes 12582928 | tf_op jit(solution)/shard_map/all_gather | solution.py:74
  598.0 16.7 %multiply_convert_fusion.5 = bf16[1024,768]{1,0:T(8,128)(2,1)} fusion(bf16[1024,6144]{0,1:T(8,128)(2,1)} %all-gather.7.cloned.1.call-done, bf16[6144,768]{1,0:T(8,128)(2,1)} %param.6, f32[]{:T(128)S(6)} %div.6), kind=kOutput, calls=%fused_computation.38 | convolution fusion | flops 9698279424 | bytes 23592964 | tf_op jit(solution)/shard_map/dot_general | solution.py:77
  614.8 16.8 %fusion.4 = bf16[768,6144]{0,1:T(8,128)(2,1)} fusion(bf16[1024,6144]{0,1:T(8,128)(2,1)} %all-gather.11.cloned.1.call-done, bf16[1024,768]{1,0:T(8,128)(2,1)S(1)} %copy-done.1), kind=kOutput, calls=%fused_computation.16 | convolution fusion | flops 9673113600 | bytes 23592960 | tf_op jit(solution)/shard_map/dot_general | solution.py:38
  631.5 12.7 %copy.9 = bf16[768,6144]{1,0:T(8,128)(2,1)} copy(bf16[768,6144]{0,1:T(8,128)(2,1)} %fusion.4) | data formatting | bytes 18874368
  644.2 17.3 %multiply_convert_fusion.2 = bf16[6144,768]{1,0:T(8,128)(2,1)} fusion(bf16[1024,6144]{0,1:T(8,128)(2,1)} %all-gather.7.cloned.1.call-done, bf16[1024,768]{1,0:T(8,128)(2,1)S(1)} %copy-done.2), kind=kOutput, calls=%fused_computation.10 | convolution fusion | flops 9673113600 | bytes 23592960 | tf_op jit(solution)/shard_map/dot_general | solution.py:38
  661.5 3.7 reduce-scatter.9.cloned.1.call-done
  (13 shorter events, 0.1 us)
Async XLA Ops:
  7.2 59.1 %all-gather.5.cloned.1.call-start = ((), (), s32[]{:S(2)}) async-start(), calls=%async_computation.4 | async-start | bytes 1966080 | tf_op jit(solution)/shard_map/all_gather | solution.py:59
  7.9 93.2 %all-gather.9.cloned.1.call-start = ((), (), s32[]{:S(2)}) async-start(), calls=%async_computation.7 | async-start | bytes 1966080 | tf_op jit(solution)/shard_map/all_gather | solution.py:60
  7.9 9.3 %copy-start = (bf16[768,6144]{1,0:T(8,128)(2,1)S(1)}, bf16[768,6144]{1,0:T(8,128)(2,1)}, u32[]{:S(2)}) copy-start(bf16[768,6144]{1,0:T(8,128)(2,1)} %param.5) | copy-start | bytes 28311556
  22.7 206.9 %reduce-scatter.13.cloned.1.call-start = ((), (), s32[]{:S(2)}) async-start(), calls=%async_computation.10 | async-start | bytes 14155776
  99.8 259.5 %reduce-scatter.15.cloned.1.call-start = ((), (), s32[]{:S(2)}) async-start(), calls=%async_computation.11 | async-start | bytes 14155776
  134.3 346.3 %all-gather.11.cloned.1.call-start = ((), (), s32[]{:S(2)}) async-start(), calls=%async_computation.8 | async-start | bytes 14155776 | tf_op jit(solution)/shard_map/all_gather | solution.py:93
  364.9 233.1 %all-gather.7.cloned.1.call-start = ((), (), s32[]{:S(2)}) async-start(), calls=%async_computation.5 | async-start | bytes 14155776 | tf_op jit(solution)/shard_map/all_gather | solution.py:74
  365.5 296.0 %reduce-scatter.11.cloned.1.call-start = ((), (), s32[]{:S(2)}) async-start(), calls=%async_computation.9 | async-start | bytes 1966080 | tf_op jit(solution)/shard_map/reduce_scatter | solution.py:96
  497.3 117.4 %copy-start.1 = (bf16[1024,768]{1,0:T(8,128)(2,1)S(1)}, bf16[1024,768]{1,0:T(8,128)(2,1)}, u32[]{:S(2)}) copy-start(bf16[1024,768]{1,0:T(8,128)(2,1)} %all-gather.5.cloned.1.call-done) | copy-start | bytes 4718596
  497.3 167.9 %reduce-scatter.9.cloned.1.call-start = ((), (), s32[]{:S(2)}) async-start(), calls=%async_computation.6 | async-start | bytes 1966080 | tf_op jit(solution)/shard_map/reduce_scatter | solution.py:76
  631.5 12.7 %copy-start.2 = (bf16[1024,768]{1,0:T(8,128)(2,1)S(1)}, bf16[1024,768]{1,0:T(8,128)(2,1)}, u32[]{:S(2)}) copy-start(bf16[1024,768]{1,0:T(8,128)(2,1)} %all-gather.9.cloned.1.call-done) | copy-start | bytes 4718596
Sparse Core Ops, SparseCore 0:
  9.8 33.8 all-gather.4
  45.6 31.0 all-gather.8
  100.0 129.5 reduce-scatter.12
  231.8 127.5 reduce-scatter.14
  365.1 115.5 all-gather.10
  482.6 115.3 all-gather.6
  601.6 29.1 reduce-scatter.10
  634.3 30.8 reduce-scatter.8
where the time goes:
time: 678 us; the launch traced here: 672 us
  waiting for transfers between devices  443 us (65%)
  matrix products  101 us (15%)
  local copies, waits for them, and re-layouts  50 us (7%)
  blocking collectives  42.8 us (6%)
  other arithmetic  18.4 us (3%)
  between operations  15.8 us (2%)
    unnamed x10, waiting for transfers between devices  224 us
    all_gather x1, waiting for transfers between devices, body(): grad_hidden_panel = lax.all_gather(hidden_grad, 'row', axis=0, tiled=True)  115 us
    all_gather x1, waiting for transfers between devices, body(): act_panel = lax.all_gather(act_share, 'row', axis=0, tiled=True)  100 us
    unnamed x11, local copies, waits for them, and re-layouts  50 us
    psum x1, blocking collectives, body(): lax.psum((jnp.sum(jnp.abs(up_latent.astype(jnp.float32))), jnp.sum(jnp.ab...  42.8 us
    dot_general x2, matrix products, contract_first(): lax.dot_general(left, right, (((0,), (0,)), ((), ())), preferred_element_...  34 us
    dot_general x2, matrix products, contract_last(): lax.dot_general(left, right, (((1,), (1,)), ((), ())), preferred_element_...  33.1 us
    dot_general x1, matrix products, body(): jnp.dot(sliced, up_tern, preferred_element_type=jnp.float32)  16.9 us
  transfers between devices with their start and end apart: 8, of which 5 were waited for; matrix products, arithmetic and copies ran while one was open for 24% of the time, Pallas kernels for 0%

commit v1 on v0

v1 whole, which is shorter than its diff:
```python
import math

import jax
import jax.numpy as jnp
from jax import lax
from jax.sharding import PartitionSpec as P

gelu_coef = math.sqrt(2.0 / math.pi)
in_flight = 2


def gelu_both(values):
    tanh_val = jnp.tanh(gelu_coef * (values + 0.044715 * values * values * values))
    value = 0.5 * values * (1.0 + tanh_val)
    slope = 0.5 * (1.0 + tanh_val) + 0.5 * values * (1.0 - tanh_val * tanh_val) * gelu_coef * (
        1.0 + 3.0 * 0.044715 * values * values
    )
    return value, slope


def ternary(latent, fan_in):
    limit = 0.8 * fan_in ** (-0.5)
    wide = latent.astype(jnp.float32)
    upper = jnp.where(wide > limit, 1.0, 0.0)
    lower = jnp.where(wide < -limit, 1.0, 0.0)
    return (upper - lower).astype(jnp.bfloat16)


def dot(left, right, left_dim, right_dim):
    return lax.dot_general(
        left, right, (((left_dim,), (right_dim,)), ((), ())), preferred_element_type=jnp.float32
    )


def body(tokens, up_latent, down_latent, out_grad):
    f32, bf16 = jnp.float32, jnp.bfloat16
    rows_axis = lax.axis_size("row")
    cols_axis = lax.axis_size("col")
    chips = rows_axis // 2
    block = tokens.shape[0]
    half = block // 2
    hid = up_latent.shape[1]
    cuts = max(1, 8 // cols_axis)
    width = hid // cuts
    grad_norm = 1.0 / math.sqrt(block * cols_axis)
    core = lax.rem(lax.axis_index("row"), 2)

    def partner(values):
        return lax.ppermute(values, "row", [(i, i ^ 1) for i in range(rows_axis)])

    def across(values, shift):
        if shift == 0:
            return values
        return lax.ppermute(values, "col", [(i, i ^ shift) for i in range(cols_axis)])

    def line(values, step):
        pairs = []
        for c in range(2):
            pairs.append((2 * step + c, 2 * step + 2 + c))
            last = chips - 1 - step
            pairs.append((2 * last + c, 2 * last - 2 + c))
        return lax.ppermute(values, "row", pairs)

    def own_first(values):
        return jnp.where(core == 0, values, jnp.concatenate([values[half:], values[:half]], axis=0))

    entry_total = up_latent.size * rows_axis * cols_axis
    scale_sums = lax.psum(
        (
            jnp.sum(jnp.abs(up_latent.astype(f32))),
            jnp.sum(jnp.abs(down_latent.astype(f32))),
        ),
        ("row", "col"),
    )
    up_scale = scale_sums[0] / entry_total
    down_scale = scale_sums[1] / entry_total
    up_fan = up_latent.shape[0] * rows_axis
    down_fan = hid * cols_axis
    up_tern = [ternary(up_latent[:, a * width : (a + 1) * width], up_fan) for a in range(cuts)]
    down_tern = [ternary(down_latent[a * width : (a + 1) * width], down_fan) for a in range(cuts)]

    tok = [own_first(across(tokens, j)) for j in range(cols_axis)]
    grad = [own_first(across(out_grad, j)) for j in range(cols_axis)]

    gate = []

    def row_sum(partial):
        own = partial[:half].astype(f32)
        base = (own + partner(partial[half:].astype(bf16)).astype(f32)).astype(bf16)
        if len(gate) >= in_flight:
            base, _ = lax.optimization_barrier((base, gate[-in_flight]))
        total = base.astype(f32)
        message = base
        for step in range(chips - 1):
            got = line(message, step)
            if step == 0:
                gate.append(got)
            total = total + got.astype(f32)
            message = (base.astype(f32) + got.astype(f32)).astype(bf16)
        return total

    order = [(j, a) for j in range(cols_axis) for a in range(cuts)]
    act, slope = {}, {}
    for j, a in order:
        hidden = up_scale * row_sum(dot(tok[j], up_tern[a], 1, 0))
        value, slope_f32 = gelu_both(hidden)
        value = value.astype(bf16)
        slope[j, a] = slope_f32.astype(bf16)
        act[j, a] = jnp.concatenate([value, partner(value)], axis=0)

    def to_owner(parts_of, weights, dim, scale):
        total = None
        for j in range(cols_axis):
            part = sum(dot(parts_of[j, a], weights[a], 1, dim) for a in range(cuts))
            part = across(own_first((scale * part).astype(bf16)), j).astype(f32)
            total = part if total is None else total + part
        return total.astype(bf16)

    grad_panel = jnp.concatenate(grad, axis=0)
    tok_panel = jnp.concatenate(tok, axis=0)
    output = to_owner(act, down_tern, 0, down_scale)
    down_grad = jnp.concatenate(
        [
            (
                dot(jnp.concatenate([act[j, a] for j in range(cols_axis)], axis=0), grad_panel, 0, 0)
                * grad_norm
            ).astype(bf16)
            for a in range(cuts)
        ],
        axis=0,
    )

    hidden_grad = {}
    for j in reversed(range(cols_axis)):
        for a in range(cuts):
            act_grad = down_scale * row_sum(dot(grad[j], down_tern[a], 1, 1))
            value = (act_grad * slope[j, a].astype(f32)).astype(bf16)
            hidden_grad[j, a] = jnp.concatenate([value, partner(value)], axis=0)
    in_grad = to_owner(hidden_grad, up_tern, 1, up_scale)
    up_grad = jnp.concatenate(
        [
            (
                dot(
                    tok_panel,
                    jnp.concatenate([hidden_grad[j, a] for j in range(cols_axis)], axis=0),
                    0,
                    0,
                )
                * grad_norm
            ).astype(bf16)
            for a in range(cuts)
        ],
        axis=1,
    )
    return (output, in_grad, up_grad, down_grad)


def solution(mesh):
    in_specs = (P("col", "row"), P("row", "col"), P("col", "row"), P("col", "row"))
    out_specs = (P("col", "row"), P("col", "row"), P("row", "col"), P("col", "row"))
    return jax.shard_map(body, mesh=mesh, in_specs=in_specs, out_specs=out_specs, check_vma=False)
```

time: 678 us -> 875 us (1.29)
  starting transfers between devices: 1.29 us -> 159 us
  waiting for transfers between devices: 443 us -> 341 us
  other arithmetic: 18.4 us -> 120 us
  matrix products: 101 us -> 145 us
  between operations: 15.8 us -> 4.77 us
  local copies, waits for them, and re-layouts: 50 us -> 59.9 us
    ppermute x0 -> x92, waiting for transfers between devices: none -> 341 us  [the longest x48 336 us: line(): return lax.ppermute(values, 'row', pairs)]
    unnamed x10 -> x0, waiting for transfers between devices: 224 us -> none
    all_gather x4 -> x0, waiting for transfers between devices: 215 us -> none  [the longest x1 115 us: body(): grad_hidden_panel = lax.all_gather(hidden_grad, 'row', axis=0, tiled=True)]
    ppermute x0 -> x92, starting transfers between devices: none -> 159 us  [the longest x48 135 us: line(): return lax.ppermute(values, 'row', pairs)]
    dot_general x6 -> x36, matrix products: 101 us -> 145 us  [dot(): lax.dot_general(left, right, (((left_dim,), (right_dim,)), ((), ())), pre...]
    unnamed x0 -> x12, other arithmetic: none -> 40.2 us
    slice x0 -> x32, local copies, waits for them, and re-layouts: none -> 36.6 us  [the longest x16 25.8 us: row_sum(): base = (own + partner(partial[half:].astype(bf16)).astype(f32)).astype(bf16)]
    convert_element_type x1 -> x50, other arithmetic: 3.62 us -> 34.9 us  [the longest x32 18.8 us: row_sum(): message = (base.astype(f32) + got.astype(f32)).astype(bf16)]
  transfers between devices with their start and end apart: 8 -> 92, of which waited for: 5 -> 24; matrix products, arithmetic and copies ran while one was open for 24% -> 36% of each run, Pallas kernels for 0% -> 0%
where the time goes in v1:
time: 875 us; the launch traced here: 869 us
  waiting for transfers between devices  341 us (39%)
  starting transfers between devices  159 us (18%)
  matrix products  145 us (17%)
  other arithmetic  120 us (14%)
  local copies, waits for them, and re-layouts  59.9 us (7%)
  blocking collectives  40.1 us (5%)
    ppermute x48, waiting for transfers between devices, line(): return lax.ppermute(values, 'row', pairs)  336 us
    dot_general x36, matrix products, dot(): lax.dot_general(left, right, (((left_dim,), (right_dim,)), ((), ())), pre...  145 us
    ppermute x48, starting transfers between devices, line(): return lax.ppermute(values, 'row', pairs)  135 us
    unnamed x12, other arithmetic  40.2 us
    psum x1, blocking collectives, body(): lax.psum((jnp.sum(jnp.abs(up_latent.astype(f32))), jnp.sum(jnp.abs(down_l...  40.1 us
    slice x16, local copies, waits for them, and re-layouts, row_sum(): base = (own + partner(partial[half:].astype(bf16)).astype(f32)).astype(bf16)  25.8 us
    unnamed x254, local copies, waits for them, and re-layouts  19.5 us
    convert_element_type x32, other arithmetic, row_sum(): message = (base.astype(f32) + got.astype(f32)).astype(bf16)  18.8 us
  transfers between devices with their start and end apart: 92, of which 24 were waited for; matrix products, arithmetic and copies ran while one was open for 36% of the time, Pallas kernels for 0%

profile of v1, /device:TPU:0, one launch (start us, length us, event | category | flops | bytes accessed | tf_op | source)
XLA Modules:
  0.0 869.5 jit_solution(4243013398314057293)
XLA Ops:
  10.8 9.3 %abs_reduce_fusion = f32[]{:T(128)} fusion(bf16[768,6144]{1,0:T(8,128)(2,1)} %param.5), kind=kLoop, calls=%fused_computation | loop fusion | flops 14155775 | bytes 9437188 | tf_op jit(solution)/shard_map/reduce_sum | solution.py:70
  28.4 9.2 %abs_reduce_fusion.1 = f32[]{:T(128)} fusion(bf16[6144,768]{1,0:T(8,128)(2,1)} %param.6), kind=kLoop, calls=%fused_computation.1 | loop fusion | flops 14155775 | bytes 9437188 | tf_op jit(solution)/shard_map/reduce_sum | solution.py:71
  47.3 40.1 %all-reduce = (f32[]{:T(128)}, f32[]{:T(128)}) all-reduce(f32[]{:T(128)} %abs_reduce_fusion, f32[]{:T(128)} %abs_reduce_fusion.1), channel_id=1, replica_groups=mesh['row'=8,'col'=4] {'row','col'}, use_global_device_ids=true, to_apply=%region_3.0 | all-reduce | flops 2 | bytes 16 | tf_op jit(solution)/shard_map/psum | solution.py:68
  198.5 12.9 %collective-permute-done.1 = bf16[128,3072]{1,0:T(8,128)(2,1)S(1)} collective-permute-done((bf16[128,3072]{1,0:T(8,128)(2,1)S(1)}, bf16[128,3072]{1,0:T(8,128)(2,1)S(1)}, u32[]{:S(2)}, u32[]{:S(2)}) %collective-permute-start.1) | collective-permute-done | bytes 786464 | tf_op jit(solution)/shard_map/ppermute | solution.py:62
  218.1 10.2 %collective-permute-done.6 = bf16[128,3072]{1,0:T(8,128)(2,1)S(1)} collective-permute-done((bf16[128,3072]{1,0:T(8,128)(2,1)S(1)}, bf16[128,3072]{1,0:T(8,128)(2,1)S(1)}, u32[]{:S(2)}, u32[]{:S(2)}) %collective-permute-start.6) | collective-permute-done | bytes 786464 | tf_op jit(solution)/shard_map/ppermute | solution.py:62
  233.8 11.3 %collective-permute-done.12 = bf16[128,3072]{1,0:T(8,128)(2,1)S(1)} collective-permute-done((bf16[128,3072]{1,0:T(8,128)(2,1)S(1)}, bf16[128,3072]{1,0:T(8,128)(2,1)S(1)}, u32[]{:S(2)}, u32[]{:S(2)}) %collective-permute-start.12) | collective-permute-done | bytes 786464 | tf_op jit(solution)/shard_map/ppermute | solution.py:62
  252.9 9.1 %collective-permute-done.17 = bf16[128,3072]{1,0:T(8,128)(2,1)S(1)} collective-permute-done((bf16[128,3072]{1,0:T(8,128)(2,1)S(1)}, bf16[128,3072]{1,0:T(8,128)(2,1)S(1)}, u32[]{:S(2)}, u32[]{:S(2)}) %collective-permute-start.17) | collective-permute-done | bytes 786464 | tf_op jit(solution)/shard_map/ppermute | solution.py:62
  268.2 10.7 %collective-permute-done.24 = bf16[128,3072]{1,0:T(8,128)(2,1)S(1)} collective-permute-done((bf16[128,3072]{1,0:T(8,128)(2,1)S(1)}, bf16[128,3072]{1,0:T(8,128)(2,1)S(1)}, u32[]{:S(2)}, u32[]{:S(2)}) %collective-permute-start.24) | collective-permute-done | bytes 786464 | tf_op jit(solution)/shard_map/ppermute | solution.py:62
  299.0 12.9 %collective-permute-done.36 = bf16[128,3072]{1,0:T(8,128)(2,1)S(1)} collective-permute-done((bf16[128,3072]{1,0:T(8,128)(2,1)S(1)}, bf16[128,3072]{1,0:T(8,128)(2,1)S(1)}, u32[]{:S(2)}, u32[]{:S(2)}) %collective-permute-start.36) | collective-permute-done | bytes 786464 | tf_op jit(solution)/shard_map/ppermute | solution.py:62
  312.0 15.3 %collective-permute-start.41 = (bf16[128,3072]{1,0:T(8,128)(2,1)S(1)}, bf16[128,3072]{1,0:T(8,128)(2,1)S(1)}, u32[]{:S(2)}, u32[]{:S(2)}) collective-permute-start(bf16[128,3072]{1,0:T(8,128)(2,1)S(1)} %fusion.120), channel_id=1, source_target_pairs={{0,8},{24,16},{4,12},{28,20},{1,9},{25,17},{5,13},{29,21},{2,10},{... | collective-permute-start | bytes 2359304 | tf_op jit(solution)/shard_map/ppermute | solution.py:62
  327.5 13.8 %collective-permute-start.53 = (bf16[128,3072]{1,0:T(8,128)(2,1)S(1)}, bf16[128,3072]{1,0:T(8,128)(2,1)S(1)}, u32[]{:S(2)}, u32[]{:S(2)}) collective-permute-start(bf16[128,3072]{1,0:T(8,128)(2,1)S(1)} %fusion.116), channel_id=1, source_target_pairs={{0,8},{24,16},{4,12},{28,20},{1,9},{25,17},{5,13},{29,21},{2,10},{... | collective-permute-start | bytes 2359304 | tf_op jit(solution)/shard_map/ppermute | solution.py:62
  345.3 12.5 %collective-permute-done.53 = bf16[128,3072]{1,0:T(8,128)(2,1)S(1)} collective-permute-done((bf16[128,3072]{1,0:T(8,128)(2,1)S(1)}, bf16[128,3072]{1,0:T(8,128)(2,1)S(1)}, u32[]{:S(2)}, u32[]{:S(2)}) %collective-permute-start.53) | collective-permute-done | bytes 786464 | tf_op jit(solution)/shard_map/ppermute | solution.py:62
  364.3 11.5 %collective-permute-done.64 = bf16[128,3072]{1,0:T(8,128)(2,1)S(1)} collective-permute-done((bf16[128,3072]{1,0:T(8,128)(2,1)S(1)}, bf16[128,3072]{1,0:T(8,128)(2,1)S(1)}, u32[]{:S(2)}, u32[]{:S(2)}) %collective-permute-start.64) | collective-permute-done | bytes 786464 | tf_op jit(solution)/shard_map/ppermute | solution.py:62
  382.4 11.2 %collective-permute-done.54 = bf16[128,3072]{1,0:T(8,128)(2,1)S(1)} collective-permute-done((bf16[128,3072]{1,0:T(8,128)(2,1)S(1)}, bf16[128,3072]{1,0:T(8,128)(2,1)S(1)}, u32[]{:S(2)}, u32[]{:S(2)}) %collective-permute-start.54) | collective-permute-done | bytes 786464 | tf_op jit(solution)/shard_map/ppermute | solution.py:62
  400.1 11.2 %collective-permute-done.65 = bf16[128,3072]{1,0:T(8,128)(2,1)S(1)} collective-permute-done((bf16[128,3072]{1,0:T(8,128)(2,1)S(1)}, bf16[128,3072]{1,0:T(8,128)(2,1)S(1)}, u32[]{:S(2)}, u32[]{:S(2)}) %collective-permute-start.65) | collective-permute-done | bytes 786464 | tf_op jit(solution)/shard_map/ppermute | solution.py:62
  418.4 15.3 %collective-permute-done.55 = bf16[128,3072]{1,0:T(8,128)(2,1)S(1)} collective-permute-done((bf16[128,3072]{1,0:T(8,128)(2,1)S(1)}, bf16[128,3072]{1,0:T(8,128)(2,1)S(1)}, u32[]{:S(2)}, u32[]{:S(2)}) %collective-permute-start.55) | collective-permute-done | bytes 786464 | tf_op jit(solution)/shard_map/ppermute | solution.py:62
  434.6 9.0 %collective-permute-done.66 = bf16[128,3072]{1,0:T(8,128)(2,1)S(1)} collective-permute-done((bf16[128,3072]{1,0:T(8,128)(2,1)S(1)}, bf16[128,3072]{1,0:T(8,128)(2,1)S(1)}, u32[]{:S(2)}, u32[]{:S(2)}) %collective-permute-start.66) | collective-permute-done | bytes 786464 | tf_op jit(solution)/shard_map/ppermute | solution.py:62
  444.5 12.5 %collective-permute-start.67 = (bf16[128,3072]{1,0:T(8,128)(2,1)S(1)}, bf16[128,3072]{1,0:T(8,128)(2,1)S(1)}, u32[]{:S(2)}, u32[]{:S(2)}) collective-permute-start(bf16[128,3072]{1,0:T(8,128)(2,1)S(1)} %fusion.115), channel_id=1, source_target_pairs={{0,8},{24,16},{4,12},{28,20},{1,9},{25,17},{5,13},{29,21},{2,10},{... | collective-permute-start | bytes 2359304 | tf_op jit(solution)/shard_map/ppermute | solution.py:62
  458.1 10.7 %collective-permute-start.56 = (bf16[128,3072]{1,0:T(8,128)(2,1)S(1)}, bf16[128,3072]{1,0:T(8,128)(2,1)S(1)}, u32[]{:S(2)}, u32[]{:S(2)}) collective-permute-start(bf16[128,3072]{1,0:T(8,128)(2,1)S(1)} %fusion.119), channel_id=1, source_target_pairs={{0,8},{24,16},{4,12},{28,20},{1,9},{25,17},{5,13},{29,21},{2,10},{... | collective-permute-start | bytes 2359304 | tf_op jit(solution)/shard_map/ppermute | solution.py:62
  470.8 12.5 %collective-permute-done.56 = bf16[128,3072]{1,0:T(8,128)(2,1)S(1)} collective-permute-done((bf16[128,3072]{1,0:T(8,128)(2,1)S(1)}, bf16[128,3072]{1,0:T(8,128)(2,1)S(1)}, u32[]{:S(2)}, u32[]{:S(2)}) %collective-permute-start.56) | collective-permute-done | bytes 786464 | tf_op jit(solution)/shard_map/ppermute | solution.py:62
  494.1 42.8 %collective-permute-done.69 = bf16[128,3072]{1,0:T(8,128)(2,1)} collective-permute-done((bf16[128,3072]{1,0:T(8,128)(2,1)S(1)}, bf16[128,3072]{1,0:T(8,128)(2,1)}, u32[]{:S(2)}, u32[]{:S(2)}) %collective-permute-start.69) | collective-permute-done | bytes 786464 | tf_op jit(solution)/shard_map/ppermute | solution.py:62
  545.8 45.5 %collective-permute-done.58 = bf16[128,3072]{1,0:T(8,128)(2,1)} collective-permute-done((bf16[128,3072]{1,0:T(8,128)(2,1)}, bf16[128,3072]{1,0:T(8,128)(2,1)}, u32[]{:S(2)}, u32[]{:S(2)}) %collective-permute-start.58) | collective-permute-done | bytes 786464 | tf_op jit(solution)/shard_map/ppermute | solution.py:62
  623.3 12.3 %collective-permute-done.75 = bf16[128,3072]{1,0:T(8,128)(2,1)} collective-permute-done((bf16[128,3072]{1,0:T(8,128)(2,1)S(1)}, bf16[128,3072]{1,0:T(8,128)(2,1)}, u32[]{:S(2)}, u32[]{:S(2)}) %collective-permute-start.75) | collective-permute-done | bytes 786464 | tf_op jit(solution)/shard_map/ppermute | solution.py:62
  643.8 25.5 %collective-permute-done.72 = bf16[128,3072]{1,0:T(8,128)(2,1)} collective-permute-done((bf16[128,3072]{1,0:T(8,128)(2,1)}, bf16[128,3072]{1,0:T(8,128)(2,1)}, u32[]{:S(2)}, u32[]{:S(2)}) %collective-permute-start.72) | collective-permute-done | bytes 786464 | tf_op jit(solution)/shard_map/ppermute | solution.py:62
  692.2 16.1 %collective-permute-done.79 = bf16[128,3072]{1,0:T(8,128)(2,1)} collective-permute-done((bf16[128,3072]{1,0:T(8,128)(2,1)S(1)}, bf16[128,3072]{1,0:T(8,128)(2,1)}, u32[]{:S(2)}, u32[]{:S(2)}) %collective-permute-start.79) | collective-permute-done | bytes 786464 | tf_op jit(solution)/shard_map/ppermute | solution.py:62
  715.0 26.2 %collective-permute-done.82 = bf16[128,3072]{1,0:T(8,128)(2,1)} collective-permute-done((bf16[128,3072]{1,0:T(8,128)(2,1)}, bf16[128,3072]{1,0:T(8,128)(2,1)}, u32[]{:S(2)}, u32[]{:S(2)}) %collective-permute-start.82) | collective-permute-done | bytes 786464 | tf_op jit(solution)/shard_map/ppermute | solution.py:62
  759.8 9.5 %collective-permute-done.89 = bf16[128,3072]{1,0:T(8,128)(2,1)S(1)} collective-permute-done((bf16[128,3072]{1,0:T(8,128)(2,1)S(1)}, bf16[128,3072]{1,0:T(8,128)(2,1)S(1)}, u32[]{:S(2)}, u32[]{:S(2)}) %collective-permute-start.89) | collective-permute-done | bytes 786464 | tf_op jit(solution)/shard_map/ppermute | solution.py:62
  788.4 8.6 multiply_convert_fusion.1
  799.6 9.9 %multiply_convert_fusion = bf16[3072,768]{1,0:T(8,128)(2,1)} fusion(bf16[1024,3072]{1,0:T(8,128)(2,1)} %constant_dynamic-update-slice_fusion.24, bf16[256,768]{1,0:T(8,128)(2,1)S(1)} %copy-done.105, bf16[256,768]{1,0:T(8,128)(2,1)S(1)} %copy-done.107, bf16[256,768]{1,0:T(8,128)(2,1)S(1)} %copy-done.109, bf16[256,768]{1,0:T(8,128)(2,1)S(1)} %copy-done.97), kind=kOutput, calls=%fused_computation.12 | convolution fusion | flops 4842848256 | bytes 12582912 | tf_op jit(solution)/shard_map/dot_general | solution.py:30
  811.4 8.2 multiply_convert_fusion.3
  820.5 9.8 %multiply_convert_fusion.2 = bf16[768,3072]{1,0:T(8,128)(2,1)} fusion(bf16[1024,3072]{1,0:T(8,128)(2,1)} %constant_dynamic-update-slice_fusion.8, bf16[256,768]{1,0:T(8,128)(2,1)S(1)} %copy-done.103, bf16[256,768]{1,0:T(8,128)(2,1)S(1)} %copy-done.101, bf16[256,768]{1,0:T(8,128)(2,1)S(1)} %copy-done.99, bf16[256,768]{1,0:T(8,128)(2,1)S(1)} %copy-done.95), kind=kOutput, calls=%fused_computation.14 | convolution fusion | flops 4842848256 | bytes 12582912 | tf_op jit(solution)/shard_map/dot_general | solution.py:30
  838.0 12.7 %pad_maximum_fusion.1 = bf16[6144,768]{1,0:T(8,128)(2,1)} fusion(bf16[3072,768]{1,0:T(8,128)(2,1)} %multiply_convert_fusion, bf16[3072,768]{1,0:T(8,128)(2,1)S(1)} %multiply_convert_fusion.1), kind=kLoop, calls=%fused_computation.11 | loop fusion | flops 18874368 | bytes 18874368 | tf_op jit(solution)/shard_map/concatenate | solution.py:122
  (559 shorter events, 376.4 us)
Async XLA Ops:
  0.6 94.5 %collective-permute-start.10 = (bf16[256,768]{1,0:T(8,128)(2,1)}, bf16[256,768]{1,0:T(8,128)(2,1)}, u32[]{:S(2)}, u32[]{:S(2)}) collective-permute-start(bf16[256,768]{1,0:T(8,128)(2,1)} %param.4), channel_id=1, source_target_pairs={{0,1},{1,0},{2,3},{3,2},{4,5},{5,4},{6,7},{7,6},{8,9},{9,8},{10,11... | collective-permute-start | bytes 1179656 | tf_op jit(solution)/shard_map/ppermute | solution.py:54
  3.6 106.0 %collective-permute-start.22 = (bf16[256,768]{1,0:T(8,128)(2,1)}, bf16[256,768]{1,0:T(8,128)(2,1)}, u32[]{:S(2)}, u32[]{:S(2)}) collective-permute-start(bf16[256,768]{1,0:T(8,128)(2,1)} %param.4), channel_id=1, source_target_pairs={{0,2},{1,3},{2,0},{3,1},{4,6},{5,7},{6,4},{7,5},{8,10},{9,11},{10,... | collective-permute-start | bytes 1179656 | tf_op jit(solution)/shard_map/ppermute | solution.py:54
  5.2 113.5 %collective-permute-start.34 = (bf16[256,768]{1,0:T(8,128)(2,1)}, bf16[256,768]{1,0:T(8,128)(2,1)}, u32[]{:S(2)}, u32[]{:S(2)}) collective-permute-start(bf16[256,768]{1,0:T(8,128)(2,1)} %param.4), channel_id=1, source_target_pairs={{0,3},{1,2},{2,1},{3,0},{4,7},{5,6},{6,5},{7,4},{8,11},{9,10},{10,... | collective-permute-start | bytes 1179656 | tf_op jit(solution)/shard_map/ppermute | solution.py:54
  5.2 123.1 %collective-permute-start.51 = (bf16[256,768]{1,0:T(8,128)(2,1)}, bf16[256,768]{1,0:T(8,128)(2,1)}, u32[]{:S(2)}, u32[]{:S(2)}) collective-permute-start(bf16[256,768]{1,0:T(8,128)(2,1)} %param.7), channel_id=1, source_target_pairs={{0,3},{1,2},{2,1},{3,0},{4,7},{5,6},{6,5},{7,4},{8,11},{9,10},{10,... | collective-permute-start | bytes 1179656 | tf_op jit(solution)/shard_map/ppermute | solution.py:54
  8.1 130.2 %collective-permute-start.49 = (bf16[256,768]{1,0:T(8,128)(2,1)}, bf16[256,768]{1,0:T(8,128)(2,1)}, u32[]{:S(2)}, u32[]{:S(2)}) collective-permute-start(bf16[256,768]{1,0:T(8,128)(2,1)} %param.7), channel_id=1, source_target_pairs={{0,2},{1,3},{2,0},{3,1},{4,6},{5,7},{6,4},{7,5},{8,10},{9,11},{10,... | collective-permute-start | bytes 1179656 | tf_op jit(solution)/shard_map/ppermute | solution.py:54
  95.1 53.9 %collective-permute-start.47 = (bf16[256,768]{1,0:T(8,128)(2,1)S(1)}, bf16[256,768]{1,0:T(8,128)(2,1)S(1)}, u32[]{:S(2)}, u32[]{:S(2)}) collective-permute-start(bf16[256,768]{1,0:T(8,128)(2,1)S(1)} %copy-done.66), channel_id=1, source_target_pairs={{0,1},{1,0},{2,3},{3,2},{4,5},{5,4},{6,7},{7,6},{8,9},{9,8},{10,11... | collective-permute-start | bytes 1179656 | tf_op jit(solution)/shard_map/ppermute | solution.py:54
  109.6 65.9 %collective-permute-start = (bf16[128,3072]{1,0:T(8,128)(2,1)}, bf16[128,3072]{1,0:T(8,128)(2,1)}, u32[]{:S(2)}, u32[]{:S(2)}) collective-permute-start(bf16[128,3072]{1,0:T(8,128)(2,1)} %slice.463), channel_id=1, source_target_pairs={{0,4},{4,0},{8,12},{12,8},{16,20},{20,16},{24,28},{28,24},{1,5},{5... | collective-permute-start | bytes 2359304 | tf_op jit(solution)/shard_map/ppermute | solution.py:49
  118.7 59.0 %collective-permute-start.46 = (bf16[128,3072]{1,0:T(8,128)(2,1)S(1)}, bf16[128,3072]{1,0:T(8,128)(2,1)}, u32[]{:S(2)}, u32[]{:S(2)}) collective-permute-start(bf16[128,3072]{1,0:T(8,128)(2,1)S(1)} %copy-done.78), channel_id=1, source_target_pairs={{0,4},{4,0},{8,12},{12,8},{16,20},{20,16},{24,28},{28,24},{1,5},{5... | collective-permute-start | bytes 2359304 | tf_op jit(solution)/shard_map/ppermute | solution.py:49
  128.3 51.0 %collective-permute-start.5 = (bf16[128,3072]{1,0:T(8,128)(2,1)S(1)}, bf16[128,3072]{1,0:T(8,128)(2,1)}, u32[]{:S(2)}, u32[]{:S(2)}) collective-permute-start(bf16[128,3072]{1,0:T(8,128)(2,1)S(1)} %slice.462), channel_id=1, source_target_pairs={{0,4},{4,0},{8,12},{12,8},{16,20},{20,16},{24,28},{28,24},{1,5},{5... | collective-permute-start | bytes 2359304 | tf_op jit(solution)/shard_map/ppermute | solution.py:49
  138.3 43.3 %collective-permute-start.60 = (bf16[128,3072]{1,0:T(8,128)(2,1)S(1)}, bf16[128,3072]{1,0:T(8,128)(2,1)}, u32[]{:S(2)}, u32[]{:S(2)}) collective-permute-start(bf16[128,3072]{1,0:T(8,128)(2,1)S(1)} %slice.451), channel_id=1, source_target_pairs={{0,4},{4,0},{8,12},{12,8},{16,20},{20,16},{24,28},{28,24},{1,5},{5... | collective-permute-start | bytes 2359304 | tf_op jit(solution)/shard_map/ppermute | solution.py:49
  193.8 34.5 %collective-permute-start.6 = (bf16[128,3072]{1,0:T(8,128)(2,1)S(1)}, bf16[128,3072]{1,0:T(8,128)(2,1)S(1)}, u32[]{:S(2)}, u32[]{:S(2)}) collective-permute-start(bf16[128,3072]{1,0:T(8,128)(2,1)S(1)} %fusion.126), channel_id=1, source_target_pairs={{0,8},{24,16},{4,12},{28,20},{1,9},{25,17},{5,13},{29,21},{2,10},{... | collective-permute-start | bytes 2359304 | tf_op jit(solution)/shard_map/ppermute | solution.py:62
  211.4 33.7 %collective-permute-start.12 = (bf16[128,3072]{1,0:T(8,128)(2,1)S(1)}, bf16[128,3072]{1,0:T(8,128)(2,1)S(1)}, u32[]{:S(2)}, u32[]{:S(2)}) collective-permute-start(bf16[128,3072]{1,0:T(8,128)(2,1)S(1)} %fusion.125), channel_id=1, source_target_pairs={{0,8},{24,16},{4,12},{28,20},{1,9},{25,17},{5,13},{29,21},{2,10},{... | collective-permute-start | bytes 2359304 | tf_op jit(solution)/shard_map/ppermute | solution.py:62
  228.3 33.7 %collective-permute-start.17 = (bf16[128,3072]{1,0:T(8,128)(2,1)S(1)}, bf16[128,3072]{1,0:T(8,128)(2,1)S(1)}, u32[]{:S(2)}, u32[]{:S(2)}) collective-permute-start(bf16[128,3072]{1,0:T(8,128)(2,1)S(1)} %fusion.124), channel_id=1, source_target_pairs={{0,8},{24,16},{4,12},{28,20},{1,9},{25,17},{5,13},{29,21},{2,10},{... | collective-permute-start | bytes 2359304 | tf_op jit(solution)/shard_map/ppermute | solution.py:62
  245.1 33.7 %collective-permute-start.24 = (bf16[128,3072]{1,0:T(8,128)(2,1)S(1)}, bf16[128,3072]{1,0:T(8,128)(2,1)S(1)}, u32[]{:S(2)}, u32[]{:S(2)}) collective-permute-start(bf16[128,3072]{1,0:T(8,128)(2,1)S(1)} %fusion.123), channel_id=1, source_target_pairs={{0,8},{24,16},{4,12},{28,20},{1,9},{25,17},{5,13},{29,21},{2,10},{... | collective-permute-start | bytes 2359304 | tf_op jit(solution)/shard_map/ppermute | solution.py:62
  250.7 293.7 %collective-permute-start.3 = (bf16[128,3072]{1,0:T(8,128)(2,1)}, bf16[128,3072]{1,0:T(8,128)(2,1)}, u32[]{:S(2)}, u32[]{:S(2)}) collective-permute-start(bf16[128,3072]{1,0:T(8,128)(2,1)} %fusion.2), channel_id=1, source_target_pairs={{16,24},{8,0},{20,28},{12,4},{17,25},{9,1},{21,29},{13,5},{18,26},... | collective-permute-start | bytes 2359304 | tf_op jit(solution)/shard_map/ppermute | solution.py:62
  262.0 33.7 %collective-permute-start.29 = (bf16[128,3072]{1,0:T(8,128)(2,1)S(1)}, bf16[128,3072]{1,0:T(8,128)(2,1)S(1)}, u32[]{:S(2)}, u32[]{:S(2)}) collective-permute-start(bf16[128,3072]{1,0:T(8,128)(2,1)S(1)} %fusion.122), channel_id=1, source_target_pairs={{0,8},{24,16},{4,12},{28,20},{1,9},{25,17},{5,13},{29,21},{2,10},{... | collective-permute-start | bytes 2359304 | tf_op jit(solution)/shard_map/ppermute | solution.py:62
  266.7 225.2 %collective-permute-start.8 = (bf16[128,3072]{1,0:T(8,128)(2,1)S(1)}, bf16[128,3072]{1,0:T(8,128)(2,1)S(1)}, u32[]{:S(2)}, u32[]{:S(2)}) collective-permute-start(bf16[128,3072]{1,0:T(8,128)(2,1)S(1)} %fusion.5), channel_id=1, source_target_pairs={{16,24},{8,0},{20,28},{12,4},{17,25},{9,1},{21,29},{13,5},{18,26},... | collective-permute-start | bytes 2359304 | tf_op jit(solution)/shard_map/ppermute | solution.py:62
  295.7 346.6 %collective-permute-start.14 = (bf16[128,3072]{1,0:T(8,128)(2,1)}, bf16[128,3072]{1,0:T(8,128)(2,1)}, u32[]{:S(2)}, u32[]{:S(2)}) collective-permute-start(bf16[128,3072]{1,0:T(8,128)(2,1)} %fusion.8), channel_id=1, source_target_pairs={{16,24},{8,0},{20,28},{12,4},{17,25},{9,1},{21,29},{13,5},{18,26},... | collective-permute-start | bytes 2359304 | tf_op jit(solution)/shard_map/ppermute | solution.py:62
  487.1 49.9 %collective-permute-start.69 = (bf16[128,3072]{1,0:T(8,128)(2,1)S(1)}, bf16[128,3072]{1,0:T(8,128)(2,1)}, u32[]{:S(2)}, u32[]{:S(2)}) collective-permute-start(bf16[128,3072]{1,0:T(8,128)(2,1)S(1)} %fusion.33), channel_id=1, source_target_pairs={{16,24},{8,0},{20,28},{12,4},{17,25},{9,1},{21,29},{13,5},{18,26},... | collective-permute-start | bytes 2359304 | tf_op jit(solution)/shard_map/ppermute | solution.py:62
  489.5 132.4 %collective-permute-start.19 = (bf16[128,3072]{1,0:T(8,128)(2,1)}, bf16[128,3072]{1,0:T(8,128)(2,1)}, u32[]{:S(2)}, u32[]{:S(2)}) collective-permute-start(bf16[128,3072]{1,0:T(8,128)(2,1)} %fusion.11), channel_id=1, source_target_pairs={{16,24},{8,0},{20,28},{12,4},{17,25},{9,1},{21,29},{13,5},{18,26},... | collective-permute-start | bytes 2359304 | tf_op jit(solution)/shard_map/ppermute | solution.py:62
  492.8 198.0 %collective-permute-start.26 = (bf16[128,3072]{1,0:T(8,128)(2,1)}, bf16[128,3072]{1,0:T(8,128)(2,1)}, u32[]{:S(2)}, u32[]{:S(2)}) collective-permute-start(bf16[128,3072]{1,0:T(8,128)(2,1)} %fusion.14), channel_id=1, source_target_pairs={{16,24},{8,0},{20,28},{12,4},{17,25},{9,1},{21,29},{13,5},{18,26},... | collective-permute-start | bytes 2359304 | tf_op jit(solution)/shard_map/ppermute | solution.py:62
  536.9 54.4 %collective-permute-start.58 = (bf16[128,3072]{1,0:T(8,128)(2,1)}, bf16[128,3072]{1,0:T(8,128)(2,1)}, u32[]{:S(2)}, u32[]{:S(2)}) collective-permute-start(bf16[128,3072]{1,0:T(8,128)(2,1)} %fusion.28), channel_id=1, source_target_pairs={{16,24},{8,0},{20,28},{12,4},{17,25},{9,1},{21,29},{13,5},{18,26},... | collective-permute-start | bytes 2359304 | tf_op jit(solution)/shard_map/ppermute | solution.py:62
  544.5 170.6 %collective-permute-start.31 = (bf16[128,3072]{1,0:T(8,128)(2,1)}, bf16[128,3072]{1,0:T(8,128)(2,1)}, u32[]{:S(2)}, u32[]{:S(2)}) collective-permute-start(bf16[128,3072]{1,0:T(8,128)(2,1)} %fusion.17), channel_id=1, source_target_pairs={{16,24},{8,0},{20,28},{12,4},{17,25},{9,1},{21,29},{13,5},{18,26},... | collective-permute-start | bytes 2359304 | tf_op jit(solution)/shard_map/ppermute | solution.py:62
  621.9 129.3 %collective-permute-start.38 = (bf16[128,3072]{1,0:T(8,128)(2,1)}, bf16[128,3072]{1,0:T(8,128)(2,1)}, u32[]{:S(2)}, u32[]{:S(2)}) collective-permute-start(bf16[128,3072]{1,0:T(8,128)(2,1)} %fusion.20), channel_id=1, source_target_pairs={{16,24},{8,0},{20,28},{12,4},{17,25},{9,1},{21,29},{13,5},{18,26},... | collective-permute-start | bytes 2359304 | tf_op jit(solution)/shard_map/ppermute | solution.py:62
  635.6 33.7 %collective-permute-start.72 = (bf16[128,3072]{1,0:T(8,128)(2,1)}, bf16[128,3072]{1,0:T(8,128)(2,1)}, u32[]{:S(2)}, u32[]{:S(2)}) collective-permute-start(bf16[128,3072]{1,0:T(8,128)(2,1)} %fusion.38), channel_id=1, source_target_pairs={{16,24},{8,0},{20,28},{12,4},{17,25},{9,1},{21,29},{13,5},{18,26},... | collective-permute-start | bytes 2359304 | tf_op jit(solution)/shard_map/ppermute | solution.py:62
  642.3 117.4 %collective-permute-start.43 = (bf16[128,3072]{1,0:T(8,128)(2,1)}, bf16[128,3072]{1,0:T(8,128)(2,1)}, u32[]{:S(2)}, u32[]{:S(2)}) collective-permute-start(bf16[128,3072]{1,0:T(8,128)(2,1)} %fusion.23), channel_id=1, source_target_pairs={{16,24},{8,0},{20,28},{12,4},{17,25},{9,1},{21,29},{13,5},{18,26},... | collective-permute-start | bytes 2359304 | tf_op jit(solution)/shard_map/ppermute | solution.py:62
  690.8 60.5 %collective-permute-start.86 = (bf16[128,3072]{1,0:T(8,128)(2,1)}, bf16[128,3072]{1,0:T(8,128)(2,1)}, u32[]{:S(2)}, u32[]{:S(2)}) collective-permute-start(bf16[128,3072]{1,0:T(8,128)(2,1)} %fusion.58), channel_id=1, source_target_pairs={{16,24},{8,0},{20,28},{12,4},{17,25},{9,1},{21,29},{13,5},{18,26},... | collective-permute-start | bytes 2359304 | tf_op jit(solution)/shard_map/ppermute | solution.py:62
  751.3 104.7 %collective-permute-start.77 = (bf16[256,768]{1,0:T(8,128)(2,1)}, bf16[256,768]{1,0:T(8,128)(2,1)S(1)}, u32[]{:S(2)}, u32[]{:S(2)}) collective-permute-start(bf16[256,768]{1,0:T(8,128)(2,1)} %maximum_select_fusion.13), channel_id=1, source_target_pairs={{0,1},{1,0},{2,3},{3,2},{4,5},{5,4},{6,7},{7,6},{8,9},{9,8},{10,11... | collective-permute-start | bytes 1179656 | tf_op jit(solution)/shard_map/ppermute | solution.py:54
  755.8 107.0 %collective-permute-start.21 = (bf16[256,768]{1,0:T(8,128)(2,1)}, bf16[256,768]{1,0:T(8,128)(2,1)}, u32[]{:S(2)}, u32[]{:S(2)}) collective-permute-start(bf16[256,768]{1,0:T(8,128)(2,1)} %maximum_select_fusion.3), channel_id=1, source_target_pairs={{0,1},{1,0},{2,3},{3,2},{4,5},{5,4},{6,7},{7,6},{8,9},{9,8},{10,11... | collective-permute-start | bytes 1179656 | tf_op jit(solution)/shard_map/ppermute | solution.py:54
  773.7 35.8 %collective-permute-start.87 = (bf16[128,3072]{1,0:T(8,128)(2,1)S(1)}, bf16[128,3072]{1,0:T(8,128)(2,1)S(1)}, u32[]{:S(2)}, u32[]{:S(2)}) collective-permute-start(bf16[128,3072]{1,0:T(8,128)(2,1)S(1)} %get-tuple-element.51), channel_id=1, source_target_pairs={{0,4},{4,0},{8,12},{12,8},{16,20},{20,16},{24,28},{28,24},{1,5},{5... | collective-permute-start | bytes 2359304 | tf_op jit(solution)/shard_map/ppermute | solution.py:49
  797.0 64.8 %collective-permute-start.84 = (bf16[256,768]{1,0:T(8,128)(2,1)}, bf16[256,768]{1,0:T(8,128)(2,1)S(1)}, u32[]{:S(2)}, u32[]{:S(2)}) collective-permute-start(bf16[256,768]{1,0:T(8,128)(2,1)} %maximum_select_fusion.14), channel_id=1, source_target_pairs={{0,2},{1,3},{2,0},{3,1},{4,6},{5,7},{6,4},{7,5},{8,10},{9,11},{10,... | collective-permute-start | bytes 1179656 | tf_op jit(solution)/shard_map/ppermute | solution.py:54
  809.5 53.4 %collective-permute-start.33 = (bf16[256,768]{1,0:T(8,128)(2,1)}, bf16[256,768]{1,0:T(8,128)(2,1)S(1)}, u32[]{:S(2)}, u32[]{:S(2)}) collective-permute-start(bf16[256,768]{1,0:T(8,128)(2,1)} %maximum_select_fusion.5), channel_id=1, source_target_pairs={{0,2},{1,3},{2,0},{3,1},{4,6},{5,7},{6,4},{7,5},{8,10},{9,11},{10,... | collective-permute-start | bytes 1179656 | tf_op jit(solution)/shard_map/ppermute | solution.py:54
  (181 other events, 2424.8 us)

commit v2 on v0

v2 whole, which is shorter than its diff:
```python
import functools
import math

import jax
import jax.numpy as jnp
from jax import lax
from jax.experimental import pallas as pl
from jax.experimental.pallas import tpu as pltpu
from jax.sharding import PartitionSpec as P

gelu_coef = math.sqrt(2.0 / math.pi)
f32, bf16 = jnp.float32, jnp.bfloat16
x_depth = 4
act_depth = 4


def gelu_both(values):
    square = values * values
    tanh_val = jnp.tanh(gelu_coef * (values + 0.044715 * square * values))
    value = 0.5 * values * (1.0 + tanh_val)
    slope = 0.5 * (1.0 + tanh_val) + 0.5 * values * (1.0 - tanh_val * tanh_val) * gelu_coef * (
        1.0 + 3.0 * 0.044715 * square
    )
    return value, slope


def ternary(latent, limit):
    wide = latent.astype(f32)
    upper = jnp.where(wide > limit, 1.0, 0.0)
    lower = jnp.where(wide < -limit, 1.0, 0.0)
    return (upper - lower).astype(bf16)


def dot(left, right, left_dim, right_dim):
    return lax.dot_general(
        left, right, (((left_dim,), (right_dim,)), ((), ())), preferred_element_type=f32
    )


def kernel(
    rows, cols, width, depth,
    tokens, up_lat, down_lat, out_grad,
    output, in_grad, up_grad, down_grad,
    tok, grad, tok_t, sums, sums_col, sums_row, base, from_left, from_right, to_right, to_left,
    x_send, x_recv, act, slope, total_out, wide_up, wide_down, act_t, down_stage, up_stage,
    part_send, part_recv,
    tok_ss, tok_rs, grad_ss, grad_rs, sc_ss, sc_rs, sr_ss, sr_rs,
    right_ss, left_rs, left_ss, right_rs, x_ss, x_rs, a_ss, a_rs, part_ss, part_rs,
    down_sem, up_sem, credit_right, credit_left, credit_x, credit_a,
):
    chips = rows // 2
    block, model = tokens.shape
    total = block * cols
    half = total // 2
    hid = up_lat.shape[1]
    cuts = hid // width
    count = 2 * cuts
    tile = 256 if model % 256 == 0 else 128
    up_limit = 0.8 * (model * rows) ** (-0.5)
    down_limit = 0.8 * (hid * cols) ** (-0.5)
    grad_norm = 1.0 / math.sqrt(total)
    me_row, me_col = lax.axis_index("row"), lax.axis_index("col")
    core = lax.rem(me_row, 2)
    z = lax.div(me_row, 2)
    mate = me_row + 1 - 2 * core
    right, left = me_row + 2, me_row - 2
    mine = pl.ds(pl.multiple_of(core * half, half), half)
    other = pl.ds(pl.multiple_of((1 - core) * half, half), half)

    def send(src, dst, send_sem, recv_sem, **where):
        return pltpu.make_async_remote_copy(
            src_ref=src, dst_ref=dst, send_sem=send_sem, recv_sem=recv_sem,
            device_id=where, device_id_type=pl.DeviceIdType.MESH,
        )

    def peer_col(k):
        return lax.rem(me_col + k, cols)

    def peer_row(k):
        return lax.rem(me_row + k, rows)

    barrier = pltpu.get_barrier_semaphore()
    for k in range(1, cols):
        pl.semaphore_signal(barrier, 1, device_id={"col": peer_col(k)}, device_id_type=pl.DeviceIdType.MESH)
    for k in range(1, rows):
        pl.semaphore_signal(barrier, 1, device_id={"row": peer_row(k)}, device_id_type=pl.DeviceIdType.MESH)
    pl.semaphore_wait(barrier, cols + rows - 2)

    own_block = pl.ds(pl.multiple_of(me_col * block, block), block)

    def panel_copy(src, panel, ss, rs, k):
        return send(src, panel.at[own_block], ss.at[k], rs.at[k], col=peer_col(k))

    for k in range(1, cols):
        panel_copy(tokens, tok, tok_ss, tok_rs, k).start()
    for k in range(1, cols):
        panel_copy(out_grad, grad, grad_ss, grad_rs, k).start()
    tok[own_block] = tokens[...]
    grad[own_block] = out_grad[...]

    def magnitudes(ref, step):
        def add(i, acc):
            piece = jnp.abs(ref[pl.ds(pl.multiple_of(i * step, step), step), :].astype(f32))
            return acc + jnp.sum(piece.reshape(step // 8, 8, piece.shape[1]), axis=0)

        acc = lax.fori_loop(0, ref.shape[0] // step, add, jnp.zeros((8, ref.shape[1]), f32))
        return sum(acc[:, k * 128 : (k + 1) * 128] for k in range(ref.shape[1] // 128))

    sums[0] = magnitudes(up_lat, 16)
    sums[1] = magnitudes(down_lat, 64)

    def exchange(slots, ss, rs, n, target):
        for k in range(1, n):
            send(sums, slots.at[k], ss.at[k], rs.at[k], **target(k)).start()
        for k in range(1, n):
            send(sums, slots.at[k], ss.at[k], rs.at[k], **target(k)).wait()
        whole = sums[...]
        for k in range(1, n):
            whole = whole + slots[k]
        sums[...] = whole

    exchange(sums_col, sc_ss, sc_rs, cols, lambda k: {"col": peer_col(k)})
    exchange(sums_row, sr_ss, sr_rs, rows, lambda k: {"row": peer_row(k)})
    entries = float(up_lat.shape[0] * up_lat.shape[1] * rows * cols)
    up_scale = jnp.sum(sums[0]) / entries
    down_scale = jnp.sum(sums[1]) / entries

    @pl.when(z == 0)
    def _():
        from_left[...] = jnp.zeros_like(from_left)

    @pl.when(z == chips - 1)
    def _():
        from_right[...] = jnp.zeros_like(from_right)

    for k in range(1, cols):
        panel_copy(tokens, tok, tok_ss, tok_rs, k).wait()
    for k in range(cols):
        tok_t[:, k * block : (k + 1) * block] = tok[k * block : (k + 1) * block, :].T

    def right_copy(c):
        return send(to_right.at[lax.rem(c, 2)], from_left.at[lax.rem(c, depth)],
                    right_ss.at[lax.rem(c, 2)], left_rs.at[lax.rem(c, depth)], row=right)

    def left_copy(c):
        return send(to_left.at[lax.rem(c, 2)], from_right.at[lax.rem(c, depth)],
                    left_ss.at[lax.rem(c, 2)], right_rs.at[lax.rem(c, depth)], row=left)

    def x_copy(c):
        return send(x_send.at[lax.rem(c, 2)], x_recv.at[lax.rem(c, x_depth)],
                    x_ss.at[lax.rem(c, 2)], x_rs.at[lax.rem(c, x_depth)], row=mate)

    def act_copy(c):
        place = act.at[lax.rem(c, act_depth), mine]
        return send(place, place, a_ss.at[lax.rem(c, act_depth)], a_rs.at[lax.rem(c, act_depth)], row=mate)

    def part_copy(which, k):
        rows_of = pl.ds(pl.multiple_of(peer_col(k) * block, block), block)
        return send(part_send.at[which, rows_of], part_recv.at[which, k],
                    part_ss.at[which, k], part_rs.at[which, k], col=peer_col(k))

    def chunk_of(c):
        return pl.ds(pl.multiple_of(c * width, width), width)

    def down_copy(c):
        return pltpu.make_async_copy(down_stage.at[lax.rem(c, 2)], down_grad.at[chunk_of(c)], down_sem.at[lax.rem(c, 2)])

    def up_copy(c):
        return pltpu.make_async_copy(up_stage.at[lax.rem(c, 2)], up_grad.at[:, chunk_of(c)], up_sem.at[lax.rem(c, 2)])

    def valid(c):
        return (c >= 0) & (c < count)

    def credit(sem, device):
        pl.semaphore_signal(sem, 1, device_id={"row": device}, device_id_type=pl.DeviceIdType.MESH)

    def partial(c, left_ref, wide, right_dim):
        slot = lax.rem(c, depth)

        @pl.loop(0, half // block)
        def _(r):
            at = pl.multiple_of(r * block, block)
            own_rows = left_ref[pl.ds(pl.multiple_of(core * half + at, block), block), :]
            base[slot, pl.ds(at, block), :] = dot(own_rows, wide[...], 1, right_dim).astype(bf16)
            mate_rows = left_ref[pl.ds(pl.multiple_of((1 - core) * half + at, block), block), :]
            x_send[lax.rem(c, 2), pl.ds(at, block), :] = dot(mate_rows, wide[...], 1, right_dim).astype(bf16)

    def accumulate(c, first, wide, right_dim):
        slot = lax.rem(c, act_depth)

        @pl.when(first)
        def _():
            @pl.loop(0, cols)
            def _(r):
                at = pl.ds(pl.multiple_of(r * block, block), block)
                total_out[at, :] = dot(act[slot, at, :], wide[...], 1, right_dim)

        @pl.when(jnp.logical_not(first))
        def _():
            @pl.loop(0, cols)
            def _(r):
                at = pl.ds(pl.multiple_of(r * block, block), block)
                total_out[at, :] += dot(act[slot, at, :], wide[...], 1, right_dim)

    def finish(which, scale):
        @pl.loop(0, cols)
        def _(r):
            at = pl.ds(pl.multiple_of(r * block, block), block)
            part_send[which, at, :] = (scale * total_out[at, :]).astype(bf16)

        for k in range(1, cols):
            part_copy(which, k).start()

    def step(i, carry):
        s = i - 1
        c_right = s - 2 - 2 * z
        c_left = s - 2 - 2 * (chips - 1 - z)
        c_act = s - 2 * chips
        has_right, has_left = z < chips - 1, z > 0

        @pl.when(valid(c_right) & has_right)
        def _():
            @pl.when(c_right >= depth)
            def _():
                pl.semaphore_wait(credit_right, 1)

            right_copy(c_right).start()

        @pl.when(valid(c_left) & has_left)
        def _():
            @pl.when(c_left >= depth)
            def _():
                pl.semaphore_wait(credit_left, 1)

            left_copy(c_left).start()

        @pl.when(valid(s))
        def _():
            @pl.when(s >= x_depth)
            def _():
                pl.semaphore_wait(credit_x, 1)

            x_copy(s).start()

        @pl.when(valid(c_act))
        def _():
            @pl.when(c_act >= act_depth)
            def _():
                pl.semaphore_wait(credit_a, 1)

            act_copy(c_act).start()

        c = s + 1

        @pl.when((s >= 1) & (s - 1 < count))
        def _():
            x_copy(s - 1).wait_send()

        @pl.when(c < cuts)
        def _():
            wide_up[...] = ternary(up_lat[:, chunk_of(c)], up_limit)
            partial(c, tok, wide_up, 0)

        @pl.when(s == min(2, cuts - 1))
        def _():
            for k in range(1, cols):
                panel_copy(out_grad, grad, grad_ss, grad_rs, k).wait()

        @pl.when((c >= cuts) & (c < count))
        def _():
            wide_down[...] = ternary(down_lat[chunk_of(c - cuts), :], down_limit)
            partial(c, grad, wide_down, 1)

        c_mul = s - 2 * chips - 1

        @pl.when(valid(c_mul))
        def _():
            act_copy(c_mul).wait()
            slot = lax.rem(c_mul, act_depth)

            @pl.when(c_mul < cuts)
            def _():
                wide_down[...] = ternary(down_lat[chunk_of(c_mul), :], down_limit)
                accumulate(c_mul, c_mul == 0, wide_down, 0)

                @pl.when(c_mul >= 2)
                def _():
                    down_copy(c_mul - 2).wait()

                @pl.loop(0, cols)
                def _(r):
                    at = pl.ds(pl.multiple_of(r * block, block), block)
                    act_t[:, at] = act[slot, at, :].T

                @pl.loop(0, model // tile)
                def _(r):
                    at = pl.ds(pl.multiple_of(r * tile, tile), tile)
                    down_stage[lax.rem(c_mul, 2), :, at] = (dot(act_t[...], grad[:, at], 1, 0) * grad_norm).astype(bf16)

                down_copy(c_mul).start()

            @pl.when(c_mul == cuts - 1)
            def _():
                finish(0, down_scale)

            @pl.when(c_mul >= cuts)
            def _():
                c_up = c_mul - cuts
                wide_up[...] = ternary(up_lat[:, chunk_of(c_up)], up_limit)
                accumulate(c_mul, c_up == 0, wide_up, 1)

                @pl.when(c_up >= 2)
                def _():
                    up_copy(c_up - 2).wait()

                @pl.loop(0, model // tile)
                def _(r):
                    at = pl.ds(pl.multiple_of(r * tile, tile), tile)
                    up_stage[lax.rem(c_up, 2), at, :] = (dot(tok_t[at, :], act[slot], 1, 0) * grad_norm).astype(bf16)

                up_copy(c_up).start()

            @pl.when(c_mul == count - 1)
            def _():
                finish(1, up_scale)

            @pl.when(c_mul + act_depth < count)
            def _():
                credit(credit_a, mate)

        @pl.when(valid(c_right - 1) & has_right)
        def _():
            right_copy(c_right - 1).wait_send()

        @pl.when(valid(c_left - 1) & has_left)
        def _():
            left_copy(c_left - 1).wait_send()

        c_base = s - 1

        @pl.when(valid(c_base))
        def _():
            x_copy(c_base).wait_recv()
            slot = lax.rem(c_base, depth)
            both = (base[slot].astype(f32) + x_recv[lax.rem(c_base, x_depth)].astype(f32)).astype(bf16)
            base[slot] = both

            @pl.when(z == 0)
            def _():
                to_right[lax.rem(c_base, 2)] = both

            @pl.when(z == chips - 1)
            def _():
                to_left[lax.rem(c_base, 2)] = both

            @pl.when(c_base + x_depth < count)
            def _():
                credit(credit_x, mate)

        c_from_left = s - 1 - 2 * z

        @pl.when(valid(c_from_left) & has_left)
        def _():
            right_copy(c_from_left).wait_recv()

            @pl.when(has_right)
            def _():
                slot = lax.rem(c_from_left, depth)
                to_right[lax.rem(c_from_left, 2)] = (
                    base[slot].astype(f32) + from_left[slot].astype(f32)
                ).astype(bf16)

        c_from_right = s - 1 - 2 * (chips - 1 - z)

        @pl.when(valid(c_from_right) & has_right)
        def _():
            left_copy(c_from_right).wait_recv()

            @pl.when(has_left)
            def _():
                slot = lax.rem(c_from_right, depth)
                to_left[lax.rem(c_from_right, 2)] = (
                    base[slot].astype(f32) + from_right[slot].astype(f32)
                ).astype(bf16)

        c_sum = s - (2 * chips - 1)

        @pl.when(valid(c_sum))
        def _():
            slot = lax.rem(c_sum, depth)
            aslot = lax.rem(c_sum, act_depth)

            @pl.loop(0, half // 64)
            def _(r):
                at = pl.ds(pl.multiple_of(r * 64, 64), 64)
                out_at = pl.ds(pl.multiple_of(core * half + r * 64, 64), 64)
                whole = (
                    base[slot, at, :].astype(f32)
                    + from_left[slot, at, :].astype(f32)
                    + from_right[slot, at, :].astype(f32)
                )

                @pl.when(c_sum < cuts)
                def _():
                    value, slope_value = gelu_both(up_scale * whole)
                    act[aslot, out_at, :] = value.astype(bf16)
                    slope[c_sum, at, :] = slope_value.astype(bf16)

                @pl.when(c_sum >= cuts)
                def _():
                    act[aslot, out_at, :] = (
                        down_scale * whole * slope[c_sum - cuts, at, :].astype(f32)
                    ).astype(bf16)

            @pl.when((c_sum + depth < count) & has_left)
            def _():
                credit(credit_right, left)

            @pl.when((c_sum + depth < count) & has_right)
            def _():
                credit(credit_left, right)

        return carry

    lax.fori_loop(0, count + 2 * chips + 2, step, 0)

    for c in range(max(0, cuts - 2), cuts):
        down_copy(c).wait()
        up_copy(c).wait()
    for which, scale, out in ((0, down_scale, output), (1, up_scale, in_grad)):
        for k in range(1, cols):
            part_copy(which, k).wait()
        result = part_send[which, own_block, :].astype(f32)
        for k in range(1, cols):
            result = result + part_recv[which, k].astype(f32)
        out[...] = result.astype(bf16)


def body(tokens, up_latent, down_latent, out_grad):
    rows, cols = lax.axis_size("row"), lax.axis_size("col")
    block, model = tokens.shape
    total, hid = block * cols, up_latent.shape[1]
    half = total // 2
    width = 256
    depth = rows + 1
    cuts = hid // width
    vmem = pl.BlockSpec(memory_space=pltpu.VMEM)
    anywhere = pl.BlockSpec(memory_space=pl.ANY)
    dma = pltpu.SemaphoreType.DMA
    scratch = [
        pltpu.VMEM((total, model), bf16),
        pltpu.VMEM((total, model), bf16),
        pltpu.VMEM((model, total), bf16),
        pltpu.VMEM((2, 8, 128), f32),
        pltpu.VMEM((cols, 2, 8, 128), f32),
        pltpu.VMEM((rows, 2, 8, 128), f32),
        pltpu.VMEM((depth, half, width), bf16),
        pltpu.VMEM((depth, half, width), bf16),
        pltpu.VMEM((depth, half, width), bf16),
        pltpu.VMEM((2, half, width), bf16),
        pltpu.VMEM((2, half, width), bf16),
        pltpu.VMEM((2, half, width), bf16),
        pltpu.VMEM((x_depth, half, width), bf16),
        pltpu.VMEM((act_depth, total, width), bf16),
        pltpu.VMEM((cuts, half, width), bf16),
        pltpu.VMEM((total, model), f32),
        pltpu.VMEM((model, width), bf16),
        pltpu.VMEM((width, model), bf16),
        pltpu.VMEM((width, total), bf16),
        pltpu.VMEM((2, width, model), bf16),
        pltpu.VMEM((2, model, width), bf16),
        pltpu.VMEM((2, total, model), bf16),
        pltpu.VMEM((2, cols, block, model), bf16),
        dma((cols,)), dma((cols,)), dma((cols,)), dma((cols,)),
        dma((cols,)), dma((cols,)), dma((rows,)), dma((rows,)),
        dma((2,)), dma((depth,)), dma((2,)), dma((depth,)),
        dma((2,)), dma((x_depth,)), dma((act_depth,)), dma((act_depth,)),
        dma((2, cols)), dma((2, cols)),
        dma((2,)), dma((2,)),
        pltpu.SemaphoreType.REGULAR,
        pltpu.SemaphoreType.REGULAR,
        pltpu.SemaphoreType.REGULAR,
        pltpu.SemaphoreType.REGULAR,
    ]
    return pl.pallas_call(
        functools.partial(kernel, rows, cols, width, depth),
        out_shape=(
            jax.ShapeDtypeStruct(tokens.shape, bf16),
            jax.ShapeDtypeStruct(tokens.shape, bf16),
            jax.ShapeDtypeStruct(up_latent.shape, bf16),
            jax.ShapeDtypeStruct(down_latent.shape, bf16),
        ),
        in_specs=[vmem] * 4,
        out_specs=(vmem, vmem, anywhere, anywhere),
        scratch_shapes=scratch,
        compiler_params=pltpu.CompilerParams(
            collective_id=0, has_side_effects=True, vmem_limit_bytes=63 * 1024 * 1024
        ),
        cost_estimate=pl.CostEstimate(
            flops=12 * total * model * hid, bytes_accessed=8 * model * hid, transcendentals=half * hid
        ),
    )(tokens, up_latent, down_latent, out_grad)


def solution(mesh):
    in_specs = (P("col", "row"), P("row", "col"), P("col", "row"), P("col", "row"))
    out_specs = (P("col", "row"), P("col", "row"), P("row", "col"), P("col", "row"))
    return jax.shard_map(body, mesh=mesh, in_specs=in_specs, out_specs=out_specs, check_vma=False)
```

time: 678 us -> 392 us (0.58)
  waiting for transfers between devices: 443 us -> 0 us
  Pallas kernels: 0 us -> 371 us
  matrix products: 101 us -> 0 us
  blocking collectives: 42.8 us -> 0 us
  local copies, waits for them, and re-layouts: 50 us -> 20.2 us
  other arithmetic: 18.4 us -> 0 us
  between operations: 15.8 us -> 0.64 us
    pallas_call x0 -> x1, Pallas kernels: none -> 371 us  [body(): pl.pallas_call(functools.partial(kernel, rows, cols, width, depth), out_s...]
    unnamed x10 -> x0, waiting for transfers between devices: 224 us -> none
    all_gather x4 -> x0, waiting for transfers between devices: 215 us -> none  [the longest x1 115 us: body(): grad_hidden_panel = lax.all_gather(hidden_grad, 'row', axis=0, tiled=True)]
    dot_general x6 -> x0, matrix products: 101 us -> none  [the longest x2 34 us: contract_first(): lax.dot_general(left, right, (((0,), (0,)), ((), ())), preferred_element_...]
    psum x1 -> x0, blocking collectives: 42.8 us -> none  [body(): lax.psum((jnp.sum(jnp.abs(up_latent.astype(jnp.float32))), jnp.sum(jnp.ab...]
    unnamed x11 -> x4, local copies, waits for them, and re-layouts: 50 us -> 20.2 us
    reduce_sum x2 -> x0, other arithmetic: 14.7 us -> none  [the longest x1 9.29 us: body(): jnp.sum(jnp.abs(down_latent.astype(jnp.float32)))]
  transfers between devices with their start and end apart: 8 -> 0, of which waited for: 5 -> 0; matrix products, arithmetic and copies ran while one was open for 24% -> 0% of each run, Pallas kernels for 0% -> 0%
where the time goes in v2:
time: 392 us
  Pallas kernels  371 us (95%)
  local copies, waits for them, and re-layouts  20.2 us (5%)
    pallas_call x1, Pallas kernels, body(): pl.pallas_call(functools.partial(kernel, rows, cols, width, depth), out_s...  371 us
    unnamed x4, local copies, waits for them, and re-layouts  20.2 us

profile of v2, /device:TPU:0, one launch (start us, length us, event | category | flops | bytes accessed | tf_op | source)
XLA Modules:
  0.0 391.8 jit_solution(16805205301102640016)
XLA Ops:
  0.6 371.0 %shard_map.75 = (bf16[256,768]{1,0:T(8,128)(2,1)}, bf16[256,768]{1,0:T(8,128)(2,1)}, bf16[768,6144]{1,0:T(8,128)(2,1)}, bf16[6144,768]{1,0:T(8,128)(2,1)}) custom-call(bf16[256,768]{1,0:T(8,128)(2,1)} %tokens.1, bf16[768,6144]{1,0:T(8,128)(2,1)} %up_lat.1, bf16[6144,768]{1,0:T(8,128)(2,1)} %down_lat.1, bf16[256,768]{1,0:T(8,128)(2,1)} %out_grad.1), custom_call_target="tpu_custom_call" | custom-call | flops 57982058496 | bytes 37748736 | tf_op jit(solution)/shard_map/pallas_call | solution.py:485
  371.7 1.8 copy.12
  373.5 1.8 copy.13
  375.2 8.6 %copy.14 = bf16[768,6144]{1,0:T(8,128)(2,1)} copy(bf16[768,6144]{1,0:T(8,128)(2,1)} %get-tuple-element.10) | data formatting | bytes 18874368
  383.8 8.0 %copy.15 = bf16[6144,768]{1,0:T(8,128)(2,1)} copy(bf16[6144,768]{1,0:T(8,128)(2,1)} %get-tuple-element.11) | data formatting | bytes 18874368
